TPU v7x, 32 devices: a whole 2x2x4 slice. The times are simulated.
32 devices in a mesh: dp: 4 (over y, x), row: 4 (over z), col: 2 (over core).
Axes of the slice: x: 2, y: 2, z: 4, core: 2. Of those that a mesh axis runs over, the one named last changes fastest.
Arguments:
- inputs: bfloat16 [576, 16384], P('row', ('dp', 'col')), may hold values from -6 to 6
- cotangent: bfloat16 [576, 16384], P('row', ('dp', 'col')), may hold values from -6 to 6
- segments: int32 [16384], P(('dp', 'row')), may hold values from 0 to 2, as said below
- positions: int32 [16384], P(('dp', 'row')), may hold values from 0 to 1021, as said below
- attn_gain: float32 [2, 576], P(None, 'row'), may hold values from 0.5 to 1.5
- w_query: bfloat16 [2, 576, 576], P(None, 'row', 'col'), may hold values from -0.25 to 0.25
- w_key: bfloat16 [2, 576, 192], P(None, 'row', 'col'), may hold values from -0.25 to 0.25
- w_value: bfloat16 [2, 576, 192], P(None, 'row', 'col'), may hold values from -0.25 to 0.25
- w_out: bfloat16 [2, 576, 576], P(None, 'col', 'row'), may hold values from -2 to 2
- ff_gain: float32 [2, 576], P(None, 'row'), may hold values from 0.5 to 1.5
- w_gate: bfloat16 [2, 576, 1536], P(None, 'row', 'col'), may hold values from -0.25 to 0.25
- w_up: bfloat16 [2, 576, 1536], P(None, 'row', 'col'), may hold values from -0.25 to 0.25
- w_down: bfloat16 [2, 1536, 576], P(None, 'col', 'row'), may hold values from -0.15625 to 0.15625
Outputs:
- outputs: bfloat16 [576, 16384], P('row', ('dp', 'col'))
- input_grad: float32 [576, 16384], P('row', ('dp', 'col'))
- attn_gain_grad: float32 [2, 576], P(None, 'row')
- query_grad: float32 [2, 576, 576], P(None, 'row', 'col')
- key_grad: float32 [2, 576, 192], P(None, 'row', 'col')
- value_grad: float32 [2, 576, 192], P(None, 'row', 'col')
- out_grad: float32 [2, 576, 576], P(None, 'col', 'row')
- ff_gain_grad: float32 [2, 576], P(None, 'row')
- gate_grad: float32 [2, 576, 1536], P(None, 'row', 'col')
- up_grad: float32 [2, 576, 1536], P(None, 'row', 'col')
- down_grad: float32 [2, 1536, 576], P(None, 'col', 'row')
Inputs may be any that keep to these rules, and one draw needn't show every extreme that they name: `segments`: segment numbers count documents within each sequence of 1024 consecutive tokens and never fall there; every sequence holds three documents, the first and the last with 1 to 256 tokens. `positions`: the position of a token within its document: 0 at each document's first token, rising by one.
All inputs are finite; a program needn't handle non-finite values.
Results may differ from a plain program's by a relative error of at most 0.02.
Values may be sent and summed in bfloat16 or wider, within the bound.
No kernel may reach another device: no remote copies, remote signals or barrier semaphores. Data moves between devices by JAX's collectives and lax.ppermute only.
A program may use at most 640 MiB of HBM per device.

v0:
```python
import functools

import jax
import jax.numpy as jnp
from jax import lax
from jax.experimental import pallas as pl
from jax.experimental.pallas import tpu as pltpu
from jax.sharding import PartitionSpec as P

D = 576
H = 9
KVH = 3
HD = 64
GROUP = H // KVH

EPSILON = 1e-05
ROTARY_BASE = 100000.0
NEGATIVE = -1e30
BF = jnp.bfloat16
F32 = jnp.float32

ORDER = ((0, 3, 1, 2), (1, 2, 0, 3))
REACH = ((((0, 1),), ((0, 4),)), (((0, 1), (2, 3)), ((0, 3),)))

def mm(left, right, left_dim, right_dim):
    return lax.dot_general(left, right, (((left_dim,), (right_dim,)), ((), ())), preferred_element_type=F32)

def fill_bias(core, start_ref, bias_ref, quarter):
    for block in range(2):
        cols = slice(block * quarter, (block + 1) * quarter)
        query_place = lax.broadcasted_iota(jnp.int32, (quarter, quarter), 1) + ORDER[core][block] * quarter
        for begin, end in REACH[core][block]:
            for part in range(begin, end):
                key_place = lax.broadcasted_iota(jnp.int32, (quarter, quarter), 0) + ORDER[core][part] * quarter
                allowed = (key_place <= query_place) & (key_place >= start_ref[:, cols])
                bias_ref[part * quarter : (part + 1) * quarter, cols] = jnp.where(allowed, 0.0, NEGATIVE)

def forward_kernel(core_ref, start_ref, query_ref, key_ref, value_ref, mixture_ref, mixed_ref, total_ref, bias_ref, turned_ref):
    quarter = query_ref.shape[1] // 2
    turned_ref[...] = key_ref[...].T

    def branch(core):
        @pl.when(pl.program_id(0) == 0)
        def _():
            fill_bias(core, start_ref, bias_ref, quarter)

        def head(number, carry):
            rows = pl.ds(number * HD, HD)
            for block in range(2):
                cols = slice(block * quarter, (block + 1) * quarter)
                query = query_ref[rows, cols]
                spans = [slice(b * quarter, e * quarter) for b, e in REACH[core][block]]
                scores = [mm(turned_ref[span, :], query, 1, 0) + bias_ref[span, cols] for span in spans]
                largest = functools.reduce(jnp.maximum, [jnp.max(s, axis=0, keepdims=True) for s in scores])
                raised = [jnp.exp(s - largest) for s in scores]
                total = sum(jnp.sum(r, axis=0, keepdims=True) for r in raised)
                mixture = sum(mm(value_ref[:, span], r.astype(BF), 1, 0) for span, r in zip(spans, raised))
                mixture = mixture / total
                mixture_ref[rows, cols] = mixture
                mixed_ref[rows, cols] = mixture.astype(BF)
                total_ref[pl.ds(number, 1), cols] = largest + jnp.log(total)
            return carry
        lax.fori_loop(0, GROUP, head, 0)

    pl.when(core_ref[0] == 0)(lambda: branch(0))
    pl.when(core_ref[0] != 0)(lambda: branch(1))

def attend(core, starts, query, key_values):
    tokens = query.shape[1]
    spec = lambda rows, count: pl.BlockSpec((rows, count), lambda g, c: (g, 0))
    return pl.pallas_call(
        forward_kernel,
        out_shape=(jax.ShapeDtypeStruct((H * HD, tokens), F32), jax.ShapeDtypeStruct((H * HD, tokens), BF), jax.ShapeDtypeStruct((KVH, 8, tokens), F32)),
        grid_spec=pltpu.PrefetchScalarGridSpec(
            num_scalar_prefetch=1, grid=(KVH,),
            in_specs=[pl.BlockSpec((1, tokens), lambda g, c: (0, 0)), spec(GROUP * HD, tokens), spec(HD, 2 * tokens),
                      pl.BlockSpec((HD, 2 * tokens), lambda g, c: (g + KVH, 0))],
            out_specs=[spec(GROUP * HD, tokens), spec(GROUP * HD, tokens), pl.BlockSpec((None, 8, tokens), lambda g, c: (g, 0, 0))],
            scratch_shapes=[pltpu.VMEM((2 * tokens, tokens), F32), pltpu.VMEM((2 * tokens, HD), BF)],
        ),
        compiler_params=pltpu.CompilerParams(vmem_limit_bytes=40 * 2**20),
        cost_estimate=pl.CostEstimate(flops=4 * H * HD * 2 * tokens * tokens, bytes_accessed=8 * H * HD * tokens, transcendentals=H * tokens * tokens),
        name="attend",
    )(core, starts, query, key_values, key_values)

def backward_kernel(core_ref, start_ref, query_ref, key_ref, value_ref, grad_ref, mixture_ref, total_ref,
                    grad_query_ref, grad_key_ref, grad_value_ref, bias_ref, turned_key_ref, turned_value_ref):
    quarter = query_ref.shape[1] // 2
    turned_key_ref[...] = key_ref[...].T
    turned_value_ref[...] = value_ref[...].T
    grad_key_ref[...] = jnp.zeros_like(grad_key_ref)
    grad_value_ref[...] = jnp.zeros_like(grad_value_ref)

    def branch(core):
        @pl.when(pl.program_id(0) == 0)
        def _():
            fill_bias(core, start_ref, bias_ref, quarter)

        def head(number, carry):
            rows = pl.ds(number * HD, HD)
            for block in range(2):
                cols = slice(block * quarter, (block + 1) * quarter)
                query = query_ref[rows, cols]
                grad = grad_ref[rows, cols]
                delta = jnp.sum(grad.astype(F32) * mixture_ref[rows, cols], axis=0, keepdims=True)
                log_total = total_ref[pl.ds(number, 1), cols]
                grad_query = jnp.zeros((HD, quarter), F32)
                for b, e in REACH[core][block]:
                    span = slice(b * quarter, e * quarter)
                    scores = mm(turned_key_ref[span, :], query, 1, 0) + bias_ref[span, cols]
                    probs = jnp.exp(scores - log_total)
                    grad_probs = mm(turned_value_ref[span, :], grad, 1, 0)
                    grad_scores = (probs * (grad_probs - delta)).astype(BF)
                    grad_query = grad_query + mm(key_ref[:, span], grad_scores, 1, 0)
                    grad_key_ref[:, span] += mm(query, grad_scores, 1, 1)
                    grad_value_ref[:, span] += mm(grad, probs.astype(BF), 1, 1)
                grad_query_ref[rows, cols] = grad_query
            return carry
        lax.fori_loop(0, GROUP, head, 0)

    pl.when(core_ref[0] == 0)(lambda: branch(0))
    pl.when(core_ref[0] != 0)(lambda: branch(1))

def attend_back(core, starts, query, key_values, grad_mixed, mixture, log_total):
    tokens = query.shape[1]
    spec = lambda rows, count: pl.BlockSpec((rows, count), lambda g, c: (g, 0))
    return pl.pallas_call(
        backward_kernel,
        out_shape=(jax.ShapeDtypeStruct((H * HD, tokens), F32), jax.ShapeDtypeStruct((KVH * HD, 2 * tokens), F32), jax.ShapeDtypeStruct((KVH * HD, 2 * tokens), F32)),
        grid_spec=pltpu.PrefetchScalarGridSpec(
            num_scalar_prefetch=1, grid=(KVH,),
            in_specs=[pl.BlockSpec((1, tokens), lambda g, c: (0, 0)), spec(GROUP * HD, tokens), spec(HD, 2 * tokens),
                      pl.BlockSpec((HD, 2 * tokens), lambda g, c: (g + KVH, 0)), spec(GROUP * HD, tokens), spec(GROUP * HD, tokens),
                      pl.BlockSpec((None, 8, tokens), lambda g, c: (g, 0, 0))],
            out_specs=[spec(GROUP * HD, tokens), spec(HD, 2 * tokens), spec(HD, 2 * tokens)],
            scratch_shapes=[pltpu.VMEM((2 * tokens, tokens), F32), pltpu.VMEM((2 * tokens, HD), BF), pltpu.VMEM((2 * tokens, HD), BF)],
        ),
        compiler_params=pltpu.CompilerParams(vmem_limit_bytes=40 * 2**20),
        cost_estimate=pl.CostEstimate(flops=10 * H * HD * 2 * tokens * tokens, bytes_accessed=16 * H * HD * tokens, transcendentals=H * tokens * tokens),
        name="attend_back",
    )(core, starts, query, key_values, key_values, grad_mixed, mixture, log_total)


def chunk_specs(near, part):
    count, width, lanes = near.shape
    return [
        pl.BlockSpec((None, width, lanes), lambda c: (jnp.minimum(c, count - 1), 0, 0)),
        pl.BlockSpec((None, width, lanes), lambda c: (jnp.maximum(c - count, 0), 0, 0)),
    ]


def ff_forward_kernel(part, count, normed_ref, middle_ref, near_ref, far_ref, hidden_ref, kept_ref):
    step = pl.program_id(0)

    @pl.when(step == 0)
    def _():
        hidden_ref[...] = middle_ref[...]

    def work(ref):
        gate_up = mm(ref[:, : 2 * part].T, normed_ref[...], 1, 0)
        kept_ref[...] = gate_up
        gate, up = gate_up[:part], gate_up[part:]
        inner = (gate * jax.nn.sigmoid(gate) * up).astype(BF)
        hidden_ref[...] += mm(ref[:, 2 * part : 3 * part], inner, 1, 0)

    pl.when(step < count)(lambda: work(near_ref))
    pl.when(step >= count)(lambda: work(far_ref))


def ff_forward(normed, middle, near, far, part):
    width, tokens = normed.shape
    count = near.shape[0]
    whole = pl.BlockSpec((width, tokens), lambda c: (0, 0))
    return pl.pallas_call(
        functools.partial(ff_forward_kernel, part, count),
        out_shape=(
            jax.ShapeDtypeStruct((width, tokens), F32),
            jax.ShapeDtypeStruct((2 * count, 2 * part, tokens), F32),
        ),
        grid=(2 * count,),
        in_specs=[whole, whole] + chunk_specs(near, part),
        out_specs=[whole, pl.BlockSpec((None, 2 * part, tokens), lambda c: (c, 0, 0))],
        compiler_params=pltpu.CompilerParams(vmem_limit_bytes=40 * 2**20),
        cost_estimate=pl.CostEstimate(
            flops=2 * 3 * width * 2 * count * part * tokens,
            bytes_accessed=20 * 2**20,
            transcendentals=2 * count * part * tokens,
        ),
        name="ff_forward",
    )(normed, middle, near, far)


def ff_backward_kernel(part, chained, order_ref, *refs):
    normed_ref, branch_ref, kept_ref, chunk_ref = refs[:4]
    total_ref, weight_ref = refs[-2:]
    step = pl.program_id(0)

    @pl.when(step == 0)
    def _():
        total_ref[...] = refs[4][...] if chained else jnp.zeros_like(total_ref)

    gate, up = kept_ref[:part], kept_ref[part:]
    grad_inner = mm(chunk_ref[:, 2 * part : 3 * part].T, branch_ref[...], 1, 0)
    sig = jax.nn.sigmoid(gate)
    silu = gate * sig
    grad_gate = (grad_inner * up * sig * (1.0 + gate * (1.0 - sig))).astype(BF)
    grad_up = (grad_inner * silu).astype(BF)
    inner = (silu * up).astype(BF)
    grad_gu = jnp.concatenate([grad_gate, grad_up], axis=0)
    total_ref[...] += mm(chunk_ref[:, : 2 * part], grad_gu, 1, 0)
    weight_ref[:, : 2 * part] = mm(normed_ref[...], grad_gu, 1, 1).astype(BF)
    weight_ref[:, 2 * part :] = mm(branch_ref[...], inner, 1, 1).astype(BF)


def ff_backward(order, normed, branch, kept, chunks, part, first, before=None):
    width, tokens = normed.shape
    count, _, lanes = chunks.shape
    whole = pl.BlockSpec((width, tokens), lambda c, order: (0, 0))
    chained = before is not None
    return pl.pallas_call(
        functools.partial(ff_backward_kernel, part, chained),
        out_shape=(
            jax.ShapeDtypeStruct((width, tokens), F32),
            jax.ShapeDtypeStruct((count, width, 3 * part), BF),
        ),
        grid_spec=pltpu.PrefetchScalarGridSpec(
            num_scalar_prefetch=1,
            grid=(count,),
            in_specs=[
                whole,
                whole,
                pl.BlockSpec((None, 2 * part, tokens), lambda c, order: (c + first, 0, 0)),
                pl.BlockSpec((None, width, lanes), lambda c, order: (c, 0, 0)),
            ]
            + ([whole] if chained else []),
            out_specs=[
                whole,
                pl.BlockSpec((None, width, 3 * part), lambda c, order: (order[c], 0, 0)),
            ],
        ),
        compiler_params=pltpu.CompilerParams(vmem_limit_bytes=40 * 2**20),
        cost_estimate=pl.CostEstimate(
            flops=2 * 6 * width * count * part * tokens,
            bytes_accessed=16 * 2**20,
            transcendentals=count * part * tokens,
        ),
        name="ff_backward",
    )(order, normed, branch, kept, chunks, *([before] if chained else []))


def swap(value, axis, distance):
    count = lax.axis_size(axis)
    return lax.ppermute(value, axis, [(i, i ^ distance) for i in range(count)])


def row_slots(value):
    return [value] + [swap(value, "row", k) for k in range(1, lax.axis_size("row"))]


def dp_step(value, turn):
    pairs = []
    for d in range(lax.axis_size("dp")):
        for c in range(2):
            distance = 1 if c == turn else 2
            pairs.append((2 * d + c, 2 * (d ^ distance) + c))
    return lax.ppermute(value, ("dp", "col"), pairs)


def place(core, slot):
    return jnp.where((core == 0) & ((slot == 1) | (slot == 2)), 3 - slot, slot)


def spread_first(value):
    return [value, swap(value, "dp", 1), swap(value, "dp", 2)]


def spread_second(parts):
    value, near, far = parts
    half = value.shape[0] // 2
    both = jnp.concatenate([swap(far[:half], "dp", 1), swap(near[half:], "dp", 2)], axis=0)
    return [value, near, far, both]


def dp_direct(value):
    return [value] + [swap(value, "dp", k) for k in range(1, lax.axis_size("dp"))]


def dp_first(value):
    return [value, dp_step(value, 1)]


def dp_second(parts):
    both = jnp.stack(parts)
    return jnp.concatenate([both, dp_step(both, 0)], axis=0)


def dp_gather(value):
    return dp_second(dp_first(value))


def reduce_dp_first(parts):
    got = dp_step(parts[2:], 0).astype(F32)
    return [(parts[1].astype(F32) + got[1]).astype(BF), parts[0].astype(F32) + got[0]]


def reduce_dp_second(parts):
    far, own = parts
    return own + dp_step(far, 1).astype(F32)


def dot(left, right, left_dim, right_dim, kind=F32):
    return lax.dot_general(
        left, right, (((left_dim,), (right_dim,)), ((), ())), preferred_element_type=F32
    ).astype(kind)


def reduce_rows(partial):
    count = lax.axis_size("row")
    size = partial.shape[0] // count
    total = partial[:size].astype(F32)
    for k in range(1, count):
        piece = partial[k * size : (k + 1) * size].astype(BF)
        total = total + swap(piece, "row", k).astype(F32)
    return total


def rms(hidden, gain):
    scale = lax.rsqrt(jnp.sum(hidden * hidden, axis=0, keepdims=True) / D + EPSILON)
    return (hidden * scale * gain).astype(BF), scale


def rms_back(grad_normed, hidden, scale, gain):
    scaled = grad_normed * gain
    inner = jnp.sum(scaled * hidden, axis=0, keepdims=True)
    grad_hidden = scale * scaled - hidden * (scale * scale * scale * inner / D)
    grad_gain = jnp.sum(grad_normed * hidden * scale, axis=1)
    return grad_hidden, grad_gain


def rotate(values, cosine, sine, heads):
    shaped = values.astype(F32).reshape(heads, 2, HD // 2, values.shape[1])
    first, second = shaped[:, 0], shaped[:, 1]
    turned = jnp.stack([first * cosine - second * sine, second * cosine + first * sine], axis=1)
    return turned.reshape(values.shape)


def chip_pairs(rows, turn):
    half = rows // 2
    pairs = []
    for r in range(rows):
        for c in range(2):
            v = r ^ turn
            pairs.append((2 * r + c, 2 * (c * half + v // 2) + v % 2))
    return pairs


def to_tokens(block, length):
    rows = lax.axis_size("row")
    me, core = lax.axis_index("row"), lax.axis_index("col")
    quarter = length // 4
    parts = []
    for v in range(rows):
        base = (v // 2) * length
        if v % 2 == 0:
            first = block[:, base : base + quarter]
            last = block[:, base + 3 * quarter : base + length]
            parts.append(jnp.concatenate([first, last], axis=1))
        else:
            parts.append(block[:, base + quarter : base + 3 * quarter])
    stacked = jnp.stack(parts)
    arrived = []
    for turn in range(rows):
        piece = lax.dynamic_index_in_dim(stacked, me ^ turn, 0, keepdims=False)
        arrived.append(lax.ppermute(piece, ("row", "col"), chip_pairs(rows, turn)))
    arrived = jnp.stack(arrived)
    origin = 2 * (me % (rows // 2)) + core
    return jnp.concatenate(
        [
            lax.dynamic_index_in_dim(arrived, me ^ k ^ origin, 0, keepdims=False)
            for k in range(rows)
        ],
        axis=0,
    )


def from_tokens(value, length):
    rows = lax.axis_size("row")
    me, core = lax.axis_index("row"), lax.axis_index("col")
    size = value.shape[0] // rows
    origin = 2 * (me % (rows // 2)) + core
    stacked = value.reshape(rows, size, value.shape[1])
    arrived = []
    for turn in range(rows):
        piece = lax.dynamic_index_in_dim(stacked, origin ^ turn ^ me, 0, keepdims=False)
        back = [(b, a) for a, b in chip_pairs(rows, turn)]
        arrived.append(lax.ppermute(piece, ("row", "col"), back))
    arrived = jnp.stack(arrived)
    quarter = length // 4
    pieces = []
    for k in range(rows // 2):
        first = lax.dynamic_index_in_dim(arrived, me ^ (2 * k), 0, keepdims=False)
        second = lax.dynamic_index_in_dim(arrived, me ^ (2 * k + 1), 0, keepdims=False)
        pieces += [first[:, :quarter], second, first[:, quarter:]]
    return jnp.concatenate(pieces, axis=1)


def own_half(tokens, core):
    quarter = tokens.shape[-1] // 4
    first = jnp.concatenate([tokens[..., :quarter], tokens[..., 3 * quarter :]], axis=-1)
    return jnp.where(core == 0, first, tokens[..., quarter : 3 * quarter])


def tie(*values):
    return lax.optimization_barrier(values)


def split_three(value):
    high = lax.reduce_precision(value, 8, 7)
    rest = value - high
    middle = lax.reduce_precision(rest, 8, 7)
    return [high.astype(BF), middle.astype(BF), (rest - middle).astype(BF)]


def shards(
    inputs,
    cotangent,
    segments,
    positions,
    attn_gain,
    w_query,
    w_key,
    w_value,
    w_out,
    ff_gain,
    w_gate,
    w_up,
    w_down,
):
    layers = w_query.shape[0]
    core = lax.axis_index("col")
    me = lax.axis_index("row")
    replica = lax.axis_index("dp")
    replicas = lax.axis_size("dp")
    rows = lax.axis_size("row")
    length = positions.shape[0]
    tokens = length // 2
    q_width = w_query.shape[2]
    k_width = w_key.shape[2]
    f_col = w_gate.shape[2]
    f_part = f_col // replicas
    at_key, at_out, at_value = q_width, q_width + k_width, 2 * q_width + k_width
    a_col = at_value + k_width
    a_part = a_col // replicas
    ff_width = 3 * f_part
    qkv_col = q_width + 2 * k_width
    core_id = core.astype(jnp.int32)[None]

    def attn_pack(number):
        whole = jnp.concatenate(
            [w_query[number], w_key[number], w_out[number].T, w_value[number]], axis=1
        )
        return lax.dynamic_slice_in_dim(whole, replica * a_part, a_part, 1)

    def ff_pack(number):
        def part(matrix):
            return lax.dynamic_slice_in_dim(matrix, replica * f_part, f_part, 1)

        return jnp.concatenate(
            [part(w_gate[number]), part(w_up[number]), part(w_down[number].T)], axis=1
        )

    def true_rows(value):
        shaped = value.reshape(rows, -1, value.shape[-1])
        return jnp.concatenate(
            [lax.dynamic_index_in_dim(shaped, me ^ k, 0, keepdims=False) for k in range(rows)],
            axis=0,
        )

    gains = jnp.concatenate([attn_gain, ff_gain], axis=0).T
    first_pack = jnp.concatenate([attn_pack(0)] + split_three(gains), axis=1)
    first = jnp.concatenate(row_slots(first_pack), axis=0)
    gains = sum(
        first[:, a_part + 2 * layers * i : a_part + 2 * layers * (i + 1)].astype(F32)
        for i in range(3)
    )
    inputs, first_pack = tie(inputs, first_pack)
    hidden = to_tokens(inputs, length).astype(F32)
    attn_near = jnp.stack(dp_direct(first[:, :a_part]))
    pack = jnp.concatenate([ff_pack(0)] + [attn_pack(n) for n in range(1, layers)], axis=1)
    pack, first = tie(pack, first)
    block = jnp.concatenate(row_slots(pack), axis=0)

    def attn_matrix(near, far):
        both = jnp.concatenate([near, far], axis=0)
        return jnp.concatenate(
            [
                lax.dynamic_index_in_dim(
                    both, (core ^ c) * replicas + (replica ^ i), 0, keepdims=False
                )
                for c in range(2)
                for i in range(replicas)
            ],
            axis=1,
        )

    def place_rows(query, key, out, value):
        pieces = []
        for c in range(2):
            for item, width in ((query, q_width), (key, k_width), (out, q_width), (value, k_width)):
                if item is None:
                    pieces.append(jnp.zeros((width, tokens), BF))
                else:
                    pieces.append(item[c * width : (c + 1) * width])
        return jnp.concatenate(pieces, axis=0)

    def take_rows(value, begin, width):
        return jnp.concatenate(
            [value[begin : begin + width], value[a_col + begin : a_col + begin + width]], axis=0
        )

    own_pos = own_half(positions, core)
    own_place = own_half(jnp.arange(length, dtype=jnp.int32), core)
    starts = (own_place - own_pos)[None]
    frequency = ROTARY_BASE ** (-(jnp.arange(HD // 2).astype(F32) / (HD // 2)))
    angles = frequency[:, None] * own_pos.astype(F32)[None, :]
    cosine, sine = jnp.cos(angles), jnp.sin(angles)

    kept = []
    attn_w, ff_w = [], []
    attn_w.append(attn_matrix(attn_near, swap(attn_near, "col", 1)))
    ff_near = spread_first(block)
    for number in range(layers):
        gain_a = gains[:, number : number + 1]
        gain_f = gains[:, layers + number : layers + number + 1]
        normed_a, scale_a = rms(hidden, gain_a)
        qkv = dot(attn_w[number], normed_a, 0, 0, BF)
        query = rotate(take_rows(qkv, 0, q_width), cosine, sine, H)
        query = query.astype(BF) * jnp.asarray(HD**-0.5, BF)
        key = rotate(take_rows(qkv, at_key, k_width), cosine, sine, KVH).astype(BF)
        own_kv = jnp.concatenate([key, take_rows(qkv, at_value, k_width)], axis=0)
        all_kv = jnp.concatenate([own_kv, swap(own_kv, "col", 1)], axis=1)
        if number + 1 < layers:
            all_kv, pack = tie(all_kv, ff_pack(number + 1))
            block = jnp.concatenate(row_slots(pack), axis=0)
        else:
            all_kv, cotangent = tie(all_kv, cotangent)
            gradient_in = to_tokens(cotangent, length)
        mixture, mixed, log_total = attend(core_id, starts, query, all_kv)
        if number == 0:
            mixed, block, *ff_near = tie(mixed, block, *ff_near)
            near = jnp.stack(spread_second(ff_near))
            ff_w.append((near, swap(near, "col", 1)))
        placed = place_rows(None, None, mixed, None)
        middle = hidden + dot(attn_w[number], placed, 1, 0)
        if number + 1 < layers:
            middle, block = tie(middle, block)
            ff_near = spread_first(block)
        normed_f, scale_f = rms(middle, gain_f)
        layer_hidden = hidden
        hidden, gate_up = ff_forward(normed_f, middle, *ff_w[number], f_part)
        kept.append(
            (layer_hidden, scale_a, normed_a, query, all_kv, mixture, log_total, placed,
             middle, scale_f, normed_f, gate_up)
        )
        if number == 0:
            near, far = ff_w[0]
            for later in range(1, layers):
                begin = ff_width + (later - 1) * a_part
                end = begin + a_part
                attn_w.append(attn_matrix(near[:, :, begin:end], far[:, :, begin:end]))
        if number + 1 < layers:
            hidden, *ff_near = tie(hidden, *ff_near)
            near = jnp.stack(spread_second(ff_near))
            ff_w.append((near, swap(near, "col", 1)))
    outputs = from_tokens(hidden.astype(BF), length)

    gradient = gradient_in.astype(F32)
    weight_grads = [None] * layers
    gain_grads = []
    pending = None
    for number in reversed(range(layers)):
        (hidden, scale_a, normed_a, query, all_kv, mixture, log_total, placed,
         middle, scale_f, normed_f, gate_up) = kept[number]
        gain_a = gains[:, number : number + 1]
        gain_f = gains[:, layers + number : layers + number + 1]
        branch = gradient.astype(BF)
        near, far = ff_w[number]
        plain = jnp.arange(replicas, dtype=jnp.int32)

        def order(c):
            return plain ^ replica if number > 0 else place(c, plain)

        grad_normed, ff_away = ff_backward(
            order(1 - core), normed_f, branch, gate_up, far, f_part, replicas
        )
        if number == 0:
            grad_normed, attn_last = tie(grad_normed, attn_last)
            attn_last = reduce_rows(attn_last).astype(BF)
        ff_got = swap(ff_away, "col", 1)
        grad_normed, ff_own = ff_backward(
            order(core), normed_f, branch, gate_up, near, f_part, 0, grad_normed
        )
        if number == 0:
            grad_normed, pending = tie(grad_normed, pending)
            pending = lax.psum_scatter(
                true_rows(pending), "row", scatter_dimension=0, tiled=True
            )

        grad_middle, gain_f_grad = rms_back(grad_normed, middle, scale_f, gain_f)
        grad_mid = gradient + grad_middle
        branch_a = grad_mid.astype(BF)
        grad_mixed = take_rows(dot(attn_w[number], branch_a, 0, 0, BF), at_out, q_width)

        def out_dot(index, kind):
            piece = lax.dynamic_slice_in_dim(placed, index * a_col + at_out, q_width, 0)
            return dot(branch_a, piece, 1, 1, kind)

        if number + 1 == layers:
            grad_mixed, outputs = tie(grad_mixed, outputs)
        ff_sum = ff_own.astype(F32) + ff_got.astype(F32)
        if number == 0:
            out_got = swap(out_dot(1 - core, BF), "col", 1)
            out_sum = out_dot(core, F32) + out_got.astype(F32)
            grad_mixed, out_sum, ff_sum = tie(grad_mixed, out_sum, ff_sum.astype(BF))
            ff_part = reduce_dp_first(ff_sum)
        else:
            grad_mixed, pending = tie(grad_mixed, ff_sum.astype(BF))
            pending = lax.psum_scatter(pending, "dp", scatter_dimension=0, tiled=False)
        grad_query, grad_keys, grad_values = attend_back(
            core_id, starts, query, all_kv, grad_mixed, mixture, log_total
        )
        if number == 0:
            grad_query, attn_last, *ff_part = tie(grad_query, attn_last, *ff_part)
            ff_part = reduce_dp_second(ff_part)
        grad_kv = jnp.concatenate([grad_keys, grad_values], axis=0)
        kv_got = swap(grad_kv[:, tokens:].astype(BF), "col", 1)
        if number == 0:
            kv_got, out_sum = tie(kv_got, out_sum)
            out_sum = reduce_rows(out_sum).astype(BF)
        grad_kv = grad_kv[:, :tokens] + kv_got.astype(F32)
        grad_query_raw = rotate(grad_query * HD**-0.5, cosine, -sine, H).astype(BF)
        grad_key_raw = rotate(grad_kv[: KVH * HD], cosine, -sine, KVH).astype(BF)
        grad_value_raw = grad_kv[KVH * HD :].astype(BF)
        grad_qkv = place_rows(grad_query_raw, grad_key_raw, None, grad_value_raw)
        grad_normed_a = dot(attn_w[number], grad_qkv, 1, 0)
        grad_lower, gain_a_grad = rms_back(grad_normed_a, hidden, scale_a, gain_a)
        gain_grads = [gain_a_grad, gain_f_grad] + gain_grads
        gradient = grad_mid + grad_lower

        def qkv_dot(index, kind):
            def part(begin, width):
                return lax.dynamic_slice_in_dim(grad_qkv, index * a_col + begin, width, 0)

            rows_of = jnp.concatenate(
                [part(0, at_out), part(at_value, k_width)], axis=0
            )
            return dot(normed_a, rows_of, 1, 1, kind)

        if number > 0:
            away = jnp.concatenate([qkv_dot(1 - core, BF), out_dot(1 - core, BF)], axis=1)
            gradient, away = tie(gradient, away)
            own = jnp.concatenate([qkv_dot(core, F32), out_dot(core, F32)], axis=1)
            attn_last = own + swap(away, "col", 1).astype(F32)
        else:
            gain_all = jnp.concatenate(
                split_three(jnp.stack(gain_grads, axis=1))[:2], axis=1
            )
            qkv_away, gain_all, gradient = tie(qkv_dot(1 - core, BF), gain_all, gradient)
            qkv_got = swap(jnp.concatenate([qkv_away, gain_all], axis=1), "col", 1)
            early = jnp.concatenate([pending, attn_last, out_sum], axis=1)
            qkv_own = jnp.concatenate([qkv_dot(core, F32), gain_all.astype(F32)], axis=1)
            qkv_sum = reduce_rows(qkv_own + qkv_got.astype(F32))
            ff_total = reduce_rows(ff_part).astype(BF)
            ff_total, gradient, *early = tie(ff_total, gradient, *dp_first(early))
            ff_total = dp_gather(ff_total)
            early = dp_second(early)
            first_total = dp_gather(qkv_sum.astype(BF))
            last_total, middle_total = early[:, :, :ff_width], early[:, :, ff_width:]
    input_grad = from_tokens(gradient.astype(BF), length).astype(F32)

    def in_order(parts):
        return [
            lax.dynamic_index_in_dim(parts, place(core, replica ^ i), 0, keepdims=False)
            for i in range(replicas)
        ]

    ff_totals = [in_order(ff_total), in_order(last_total)]

    def ff_of(number, begin, end):
        return jnp.concatenate([p[:, begin:end] for p in ff_totals[number]], axis=1).astype(F32)

    def total_of(parts):
        parts = parts.astype(F32)
        return (parts[0] + parts[3]) + (parts[1] + parts[2])

    first_total, middle_total = total_of(first_total), total_of(middle_total)
    attn_whole = [
        jnp.concatenate([first_total[:, :qkv_col], middle_total[:, a_col:]], axis=1),
        middle_total[:, :a_col],
    ]

    def attn_of(number, begin, end):
        return attn_whole[number][:, begin:end]

    def stack(function):
        return jnp.stack([function(number) for number in range(layers)])

    gain_total = first_total[:, qkv_col:]
    gain_total = gain_total[:, : 2 * layers] + gain_total[:, 2 * layers :]
    gain_total = gain_total.T.reshape(layers, 2, -1)

    return (
        outputs,
        input_grad,
        gain_total[:, 0],
        stack(lambda n: attn_of(n, 0, q_width)),
        stack(lambda n: attn_of(n, q_width, q_width + k_width)),
        stack(lambda n: attn_of(n, q_width + k_width, qkv_col)),
        stack(lambda n: attn_of(n, qkv_col, a_col).T),
        gain_total[:, 1],
        stack(lambda n: ff_of(n, 0, f_part)),
        stack(lambda n: ff_of(n, f_part, 2 * f_part)),
        stack(lambda n: ff_of(n, 2 * f_part, ff_width).T),
    )


def solution(mesh):
    return jax.shard_map(
        shards,
        mesh=mesh,
        in_specs=(
            P("row", ("dp", "col")),
            P("row", ("dp", "col")),
            P(("dp", "row")),
            P(("dp", "row")),
            P(None, "row"),
            P(None, "row", "col"),
            P(None, "row", "col"),
            P(None, "row", "col"),
            P(None, "col", "row"),
            P(None, "row"),
            P(None, "row", "col"),
            P(None, "row", "col"),
            P(None, "col", "row"),
        ),
        out_specs=(
            P("row", ("dp", "col")),
            P("row", ("dp", "col")),
            P(None, "row"),
            P(None, "row", "col"),
            P(None, "row", "col"),
            P(None, "row", "col"),
            P(None, "col", "row"),
            P(None, "row"),
            P(None, "row", "col"),
            P(None, "row", "col"),
            P(None, "col", "row"),
        ),
        check_vma=False,
    )
```

profile of v0, /device:TPU:0, one launch (start us, length us, event | category | flops | bytes accessed | tf_op | source)
XLA Modules:
  0.0 432.6 jit_solution(12361205592870421831)
XLA Ops:
  11.9 5.1 %collective-permute-start.2 = (bf16[144,204]{0,1:T(8,128)(2,1)S(1)}, bf16[144,204]{0,1:T(8,128)(2,1)S(1)}, u32[]{:S(2)}, u32[]{:S(2)}) collective-permute-start(bf16[144,204]{0,1:T(8,128)(2,1)S(1)} %pad_maximum_fusion.44), channel_id=1, source_target_pairs={{0,6},{2,4},{4,2},{6,0},{1,7},{3,5},{5,3},{7,1},{8,14},{10,12},{12... | collective-permute-start | bytes 176264 | tf_op jit(solution)/shard_map/ppermute | solution.py:253
  18.8 4.6 %collective-permute-start.10 = (bf16[144,512]{1,0:T(8,128)(2,1)S(1)}, bf16[144,512]{1,0:T(8,128)(2,1)S(1)}, u32[]{:S(2)}, u32[]{:S(2)}) collective-permute-start(bf16[144,512]{1,0:T(8,128)(2,1)S(1)} %get-tuple-element.264), channel_id=1, source_target_pairs={{0,3},{1,7},{2,2},{3,6},{4,1},{5,5},{6,0},{7,4},{8,11},{9,15},{10,... | collective-permute-start | bytes 442376 | tf_op jit(solution)/shard_map/ppermute | solution.py:374
  35.8 7.8 %collective-permute-done.9 = bf16[144,512]{1,0:T(8,128)(2,1)S(1)} collective-permute-done((bf16[144,512]{1,0:T(8,128)(2,1)S(1)}, bf16[144,512]{1,0:T(8,128)(2,1)S(1)}, u32[]{:S(2)}, u32[]{:S(2)}) %collective-permute-start.9) | collective-permute-done | bytes 147488 | tf_op jit(solution)/shard_map/ppermute | solution.py:374
  70.8 10.3 %attend.2 = (f32[576,512]{1,0:T(8,128)S(1)}, bf16[576,512]{1,0:T(8,128)(2,1)S(1)}, f32[3,8,512]{2,1,0:T(8,128)S(1)}) custom-call(s32[1]{0:T(128)} %bitcast.core_ref, s32[1,512]{1,0:T(1,128)S(1)} %bitcast.339, bf16[576,512]{1,0:T(8,128)(2,1)S(1)} %bitcast.335, bf16[384,1024]{1,0:T(8,128)(2,1)S(1)} %pad_maximum_fusion.6.key_ref.value_ref, ...), custom_call_target="tpu_custom_call" | custom-call | flops 1207959552 | bytes 2359296 | tf_op jit(solution)/shard_map/attend/pallas_call | solution.py:71
  85.0 10.8 %collective-permute-done.20 = bf16[288,768]{1,0:T(8,128)(2,1)S(1)} collective-permute-done((bf16[288,768]{1,0:T(8,128)(2,1)S(1)}, bf16[288,768]{1,0:T(8,128)(2,1)S(1)}, u32[]{:S(2)}, u32[]{:S(2)}) %collective-permute-start.20) | collective-permute-done | bytes 442400 | tf_op jit(solution)/shard_map/ppermute | solution.py:253
  111.0 9.9 %ff_forward.2 = (f32[576,512]{1,0:T(8,128)S(1)}, f32[8,384,512]{2,1,0:T(8,128)}) custom-call(bf16[576,512]{1,0:T(8,128)(2,1)S(1)} %multiply_convert_fusion.2.normed_ref.refs_0_, f32[576,512]{1,0:T(8,128)S(1)} %convert_add_fusion.middle_ref, bf16[4,576,768]{2,1,0:T(8,128)(2,1)S(1)} %pad_maximum_fusion.near_ref.refs_3_, ...), custom_call_target="tpu_custom_call" | custom-call | flops 2717908992 | bytes 20971520 | tf_op jit(solution)/shard_map/ff_forward/pallas_call | solution.py:174
  123.3 4.3 concatenate.269
  135.5 6.6 %collective-permute-done.30 = bf16[288,576]{1,0:T(8,128)(2,1)S(1)} collective-permute-done((bf16[288,576]{1,0:T(8,128)(2,1)S(1)}, bf16[288,576]{1,0:T(8,128)(2,1)S(1)}, u32[]{:S(2)}, u32[]{:S(2)}) %collective-permute-start.30) | collective-permute-done | bytes 331808 | tf_op jit(solution)/shard_map/ppermute | solution.py:253
  151.7 10.0 %attend.3 = (f32[576,512]{1,0:T(8,128)S(1)}, bf16[576,512]{1,0:T(8,128)(2,1)S(1)}, f32[3,8,512]{2,1,0:T(8,128)S(1)}) custom-call(s32[1]{0:T(128)} %bitcast.core_ref, s32[1,512]{1,0:T(1,128)S(1)} %bitcast.340, bf16[576,512]{1,0:T(8,128)(2,1)S(1)} %bitcast.337, bf16[384,1024]{1,0:T(8,128)(2,1)S(1)} %pad_maximum_fusion.7.key_ref.value_ref, ...), custom_call_target="tpu_custom_call" | custom-call | flops 1207959552 | bytes 2359296 | tf_op jit(solution)/shard_map/attend/pallas_call | solution.py:71
  169.8 7.8 %ff_forward.3 = (f32[576,512]{1,0:T(8,128)S(1)}, f32[8,384,512]{2,1,0:T(8,128)}) custom-call(bf16[576,512]{1,0:T(8,128)(2,1)S(1)} %multiply_convert_fusion.normed_ref.refs_0_, f32[576,512]{1,0:T(8,128)S(1)} %get-tuple-element.341.middle_ref, bf16[4,576,576]{2,1,0:T(8,128)(2,1)S(1)} %pad_maximum_fusion.1.near_ref.refs_3_, ...), custom_call_target="tpu_custom_call" | custom-call | flops 2717908992 | bytes 20971520 | tf_op jit(solution)/shard_map/ff_forward/pallas_call | solution.py:174
  189.7 6.7 %ff_backward.4 = (f32[576,512]{1,0:T(8,128)S(1)}, bf16[4,576,576]{2,1,0:T(8,128)(2,1)}) custom-call(s32[4]{0:T(128)S(1)} %iota_xor_fusion.order_ref, bf16[576,512]{1,0:T(8,128)(2,1)S(1)} %multiply_convert_fusion.normed_ref.refs_0_, bf16[576,512]{1,0:T(8,128)(2,1)S(1)} %pad_maximum_fusion.18.refs_1_, f32[8,384,512]{2,1,0:T(8,128)S(1)} %copy-done, ...), custom_call_target="tpu_custom_call" | custom-call | flops 2717908992 | bytes 16777216 | tf_op jit(solution)/shard_map/ff_backward/pallas_call | solution.py:220
  196.4 6.9 %ff_backward.5 = (f32[576,512]{1,0:T(8,128)S(1)}, bf16[4,576,576]{2,1,0:T(8,128)(2,1)S(1)}) custom-call(s32[4]{0:T(128)S(1)} %iota_xor_fusion.order_ref, bf16[576,512]{1,0:T(8,128)(2,1)S(1)} %multiply_convert_fusion.normed_ref.refs_0_, bf16[576,512]{1,0:T(8,128)(2,1)S(1)} %pad_maximum_fusion.18.refs_1_, f32[8,384,512]{2,1,0:T(8,128)} %get-tuple-element.98.refs_2_, ...), custom_call_target="tpu_custom_call" | custom-call | flops 2717908992 | bytes 16777216 | tf_op jit(solution)/shard_map/ff_backward/pallas_call | solution.py:220
  216.7 4.2 add_convert_fusion.1
  226.2 10.3 %attend_back.2 = (f32[576,512]{1,0:T(8,128)S(1)}, f32[192,1024]{1,0:T(8,128)S(1)}, f32[192,1024]{1,0:T(8,128)S(1)}) custom-call(s32[1]{0:T(128)} %bitcast.core_ref, s32[1,512]{1,0:T(1,128)S(1)} %bitcast.341, bf16[576,512]{1,0:T(8,128)(2,1)S(1)} %bitcast.338, bf16[384,1024]{1,0:T(8,128)(2,1)S(1)} %copy-done.22, bf16[384,1024]{1,0:T(8,128)(2,1)S(1)} %copy-done.22, ...), custom_call_target="tpu_custom_call" | custom-call | flops 3019898880 | bytes 4718592 | tf_op jit(solution)/shard_map/attend_back/pallas_call | solution.py:127
  251.6 9.2 %ff_backward.6 = (f32[576,512]{1,0:T(8,128)S(1)}, bf16[4,576,576]{2,1,0:T(8,128)(2,1)}) custom-call(s32[4]{0:T(128)S(1)} %and_select_fusion.order_ref, bf16[576,512]{1,0:T(8,128)(2,1)S(1)} %copy-done.9, bf16[576,512]{1,0:T(8,128)(2,1)S(1)} %convert_element_type.348.refs_1_, f32[8,384,512]{2,1,0:T(8,128)} %get-tuple-element.113.refs_2_, ...), custom_call_target="tpu_custom_call" | custom-call | flops 2717908992 | bytes 16777216 | tf_op jit(solution)/shard_map/ff_backward/pallas_call | solution.py:220
  275.9 7.0 %ff_backward.7 = (f32[576,512]{1,0:T(8,128)S(1)}, bf16[4,576,576]{2,1,0:T(8,128)(2,1)S(1)}) custom-call(s32[4]{0:T(128)S(1)} %and_select_fusion.1.order_ref, bf16[576,512]{1,0:T(8,128)(2,1)S(1)} %copy-done.10, bf16[576,512]{1,0:T(8,128)(2,1)S(1)} %copy-done.7, f32[8,384,512]{2,1,0:T(8,128)} %get-tuple-element.113.refs_2_, ...), custom_call_target="tpu_custom_call" | custom-call | flops 2717908992 | bytes 16777216 | tf_op jit(solution)/shard_map/ff_backward/pallas_call | solution.py:220
  284.0 4.3 %add_convert_fusion = bf16[4,576,576]{2,1,0:T(8,128)(2,1)} fusion(bf16[4,576,576]{2,1,0:T(8,128)(2,1)} %collective-permute-done.41, bf16[4,576,576]{2,1,0:T(8,128)(2,1)S(1)} %get-tuple-element.120), kind=kLoop, calls=%fused_computation | loop fusion | flops 5308416 | bytes 7962624 | tf_op jit(solution)/shard_map/convert_element_type | solution.py:624
  298.3 10.5 %attend_back.3 = (f32[576,512]{1,0:T(8,128)S(1)}, f32[192,1024]{1,0:T(8,128)S(1)}, f32[192,1024]{1,0:T(8,128)S(1)}) custom-call(s32[1]{0:T(128)} %bitcast.core_ref, s32[1,512]{1,0:T(1,128)S(1)} %bitcast.342, bf16[576,512]{1,0:T(8,128)(2,1)S(1)} %bitcast.336, bf16[384,1024]{1,0:T(8,128)(2,1)S(1)} %copy-done.20, bf16[384,1024]{1,0:T(8,128)(2,1)S(1)} %copy-done.20, ...), custom_call_target="tpu_custom_call" | custom-call | flops 3019898880 | bytes 4718592 | tf_op jit(solution)/shard_map/attend_back/pallas_call | solution.py:127
  335.3 10.2 %collective-permute-done.52 = bf16[144,288]{0,1:T(8,128)(2,1)} collective-permute-done((bf16[144,288]{0,1:T(8,128)(2,1)}, bf16[144,288]{0,1:T(8,128)(2,1)}, u32[]{:S(2)}, u32[]{:S(2)}) %collective-permute-start.52) | collective-permute-done | bytes 82976 | tf_op jit(solution)/shard_map/ppermute | solution.py:253
  364.6 4.5 %collective-permute-start.48 = (bf16[144,576]{1,0:T(8,128)(2,1)S(1)}, bf16[144,576]{1,0:T(8,128)(2,1)S(1)}, u32[]{:S(2)}, u32[]{:S(2)}) collective-permute-start(bf16[144,576]{1,0:T(8,128)(2,1)S(1)} %get-tuple-element.224), channel_id=1, source_target_pairs={{0,4},{2,6},{4,0},{6,2},{1,5},{3,7},{5,1},{7,3},{8,12},{10,14},{12... | collective-permute-start | bytes 497672 | tf_op jit(solution)/shard_map/ppermute | solution.py:253
  369.2 8.6 %collective-permute-done.61 = bf16[144,488]{1,0:T(8,128)(2,1)S(1)} collective-permute-done((bf16[144,488]{1,0:T(8,128)(2,1)S(1)}, bf16[144,488]{1,0:T(8,128)(2,1)S(1)}, u32[]{:S(2)}, u32[]{:S(2)}) %collective-permute-start.61) | collective-permute-done | bytes 140576 | tf_op jit(solution)/shard_map/ppermute | solution.py:253
  378.7 5.4 %collective-permute-done.48 = bf16[144,576]{1,0:T(8,128)(2,1)S(1)} collective-permute-done((bf16[144,576]{1,0:T(8,128)(2,1)S(1)}, bf16[144,576]{1,0:T(8,128)(2,1)S(1)}, u32[]{:S(2)}, u32[]{:S(2)}) %collective-permute-start.48) | collective-permute-done | bytes 165920 | tf_op jit(solution)/shard_map/ppermute | solution.py:253
  384.9 5.8 %collective-permute-start.58 = (bf16[144,512]{1,0:T(8,128)(2,1)S(1)}, bf16[144,512]{1,0:T(8,128)(2,1)S(1)}, u32[]{:S(2)}, u32[]{:S(2)}) collective-permute-start(bf16[144,512]{1,0:T(8,128)(2,1)S(1)} %get-tuple-element.236), channel_id=1, source_target_pairs={{3,0},{7,1},{2,2},{6,3},{1,4},{5,5},{0,6},{4,7},{11,8},{15,9},{10,... | collective-permute-start | bytes 442376 | tf_op jit(solution)/shard_map/ppermute | solution.py:396
  401.3 10.4 %collective-permute-done.64 = bf16[2,144,488]{2,1,0:T(8,128)(2,1)S(1)} collective-permute-done((bf16[2,144,488]{2,1,0:T(8,128)(2,1)S(1)}, bf16[2,144,488]{2,1,0:T(8,128)(2,1)S(1)}, u32[]{:S(2)}, u32[]{:S(2)}) %collective-permute-start.64) | collective-permute-done | bytes 281120 | tf_op jit(solution)/shard_map/ppermute | solution.py:266
  (674 shorter events, 233.8 us)
Async XLA Ops:
  7.2 281.1 %reduce-scatter.7.cloned.1.call-start = ((), (), s32[]{:S(2)}) async-start(), calls=%async_computation.3 | async-start | bytes 3686400
  30.0 28.8 %collective-permute-start.17 = (bf16[144,768]{1,0:T(8,128)(2,1)S(1)}, bf16[144,768]{1,0:T(8,128)(2,1)S(1)}, u32[]{:S(2)}, u32[]{:S(2)}) collective-permute-start(bf16[144,768]{1,0:T(8,128)(2,1)S(1)} %pad_maximum_fusion.34), channel_id=1, source_target_pairs={{0,6},{2,4},{4,2},{6,0},{1,7},{3,5},{5,3},{7,1},{8,14},{10,12},{12... | collective-permute-start | bytes 663560 | tf_op jit(solution)/shard_map/ppermute | solution.py:253
  34.1 20.9 %collective-permute-start.15 = (bf16[144,768]{1,0:T(8,128)(2,1)S(1)}, bf16[144,768]{1,0:T(8,128)(2,1)S(1)}, u32[]{:S(2)}, u32[]{:S(2)}) collective-permute-start(bf16[144,768]{1,0:T(8,128)(2,1)S(1)} %pad_maximum_fusion.34), channel_id=1, source_target_pairs={{0,2},{2,0},{4,6},{6,4},{1,3},{3,1},{5,7},{7,5},{8,10},{10,8},{12,... | collective-permute-start | bytes 663560 | tf_op jit(solution)/shard_map/ppermute | solution.py:253
  58.8 24.8 %collective-permute-start.19 = (bf16[576,768]{1,0:T(8,128)(2,1)S(1)}, bf16[576,768]{1,0:T(8,128)(2,1)S(1)}, u32[]{:S(2)}, u32[]{:S(2)}) collective-permute-start(bf16[576,768]{1,0:T(8,128)(2,1)S(1)} %constant_dynamic-update-slice_fusion.5), channel_id=1, source_target_pairs={{0,16},{8,24},{16,0},{24,8},{1,17},{9,25},{17,1},{25,9},{2,18},{10... | collective-permute-start | bytes 2654216 | tf_op jit(solution)/shard_map/ppermute | solution.py:253
  60.4 23.3 %collective-permute-start.18 = (bf16[576,768]{1,0:T(8,128)(2,1)S(1)}, bf16[576,768]{1,0:T(8,128)(2,1)S(1)}, u32[]{:S(2)}, u32[]{:S(2)}) collective-permute-start(bf16[576,768]{1,0:T(8,128)(2,1)S(1)} %constant_dynamic-update-slice_fusion.5), channel_id=1, source_target_pairs={{0,8},{8,0},{16,24},{24,16},{1,9},{9,1},{17,25},{25,17},{2,10},{10... | collective-permute-start | bytes 2654216 | tf_op jit(solution)/shard_map/ppermute | solution.py:253
  143.8 26.1 %collective-permute-start.32 = (bf16[4,576,576]{2,1,0:T(8,128)(2,1)S(1)}, bf16[4,576,576]{2,1,0:T(8,128)(2,1)S(1)}, u32[]{:S(2)}, u32[]{:S(2)}) collective-permute-start(bf16[4,576,576]{2,1,0:T(8,128)(2,1)S(1)} %pad_maximum_fusion.1.near_ref.refs_3_), channel_id=1, source_target_pairs={{0,1},{1,0},{2,3},{3,2},{4,5},{5,4},{6,7},{7,6},{8,9},{9,8},{10,11... | collective-permute-start | bytes 7962632 | tf_op jit(solution)/shard_map/ppermute | solution.py:253
  145.1 24.5 %collective-permute-start.26 = (bf16[144,512]{1,0:T(8,128)(2,1)S(1)}, bf16[144,512]{1,0:T(8,128)(2,1)S(1)}, u32[]{:S(2)}, u32[]{:S(2)}) collective-permute-start(bf16[144,512]{1,0:T(8,128)(2,1)S(1)} %get-tuple-element.249), channel_id=1, source_target_pairs={{0,0},{1,4},{2,1},{3,5},{4,2},{5,6},{6,3},{7,7},{8,8},{9,12},{10,9... | collective-permute-start | bytes 442376 | tf_op jit(solution)/shard_map/ppermute | solution.py:374
  145.7 23.9 %collective-permute-start.29 = (bf16[144,512]{1,0:T(8,128)(2,1)S(1)}, bf16[144,512]{1,0:T(8,128)(2,1)S(1)}, u32[]{:S(2)}, u32[]{:S(2)}) collective-permute-start(bf16[144,512]{1,0:T(8,128)(2,1)S(1)} %get-tuple-element.250), channel_id=1, source_target_pairs={{0,3},{1,7},{2,2},{3,6},{4,1},{5,5},{6,0},{7,4},{8,11},{9,15},{10,... | collective-permute-start | bytes 442376 | tf_op jit(solution)/shard_map/ppermute | solution.py:374
  148.4 21.2 %collective-permute-start.28 = (bf16[144,512]{1,0:T(8,128)(2,1)S(1)}, bf16[144,512]{1,0:T(8,128)(2,1)S(1)}, u32[]{:S(2)}, u32[]{:S(2)}) collective-permute-start(bf16[144,512]{1,0:T(8,128)(2,1)S(1)} %get-tuple-element.251), channel_id=1, source_target_pairs={{0,2},{1,6},{2,3},{3,7},{4,0},{5,4},{6,1},{7,5},{8,10},{9,14},{10,... | collective-permute-start | bytes 442376 | tf_op jit(solution)/shard_map/ppermute | solution.py:374
  149.0 20.6 %collective-permute-start.27 = (bf16[144,512]{1,0:T(8,128)(2,1)S(1)}, bf16[144,512]{1,0:T(8,128)(2,1)S(1)}, u32[]{:S(2)}, u32[]{:S(2)}) collective-permute-start(bf16[144,512]{1,0:T(8,128)(2,1)S(1)} %get-tuple-element.252), channel_id=1, source_target_pairs={{0,1},{1,5},{2,0},{3,4},{4,3},{5,7},{6,2},{7,6},{8,9},{9,13},{10,8... | collective-permute-start | bytes 442376 | tf_op jit(solution)/shard_map/ppermute | solution.py:374
  178.6 35.7 %collective-permute-start.33 = (bf16[144,512]{1,0:T(8,128)(2,1)}, bf16[144,512]{1,0:T(8,128)(2,1)}, u32[]{:S(2)}, u32[]{:S(2)}) collective-permute-start(bf16[144,512]{1,0:T(8,128)(2,1)} %get-tuple-element.241), channel_id=1, source_target_pairs={{0,0},{4,1},{1,2},{5,3},{2,4},{6,5},{3,6},{7,7},{8,8},{12,9},{9,10... | collective-permute-start | bytes 442376 | tf_op jit(solution)/shard_map/ppermute | solution.py:396
  181.5 32.8 %collective-permute-start.36 = (bf16[144,512]{1,0:T(8,128)(2,1)}, bf16[144,512]{1,0:T(8,128)(2,1)}, u32[]{:S(2)}, u32[]{:S(2)}) collective-permute-start(bf16[144,512]{1,0:T(8,128)(2,1)} %get-tuple-element.242), channel_id=1, source_target_pairs={{3,0},{7,1},{2,2},{6,3},{1,4},{5,5},{0,6},{4,7},{11,8},{15,9},{10,... | collective-permute-start | bytes 442376 | tf_op jit(solution)/shard_map/ppermute | solution.py:396
  184.8 29.5 %collective-permute-start.35 = (bf16[144,512]{1,0:T(8,128)(2,1)}, bf16[144,512]{1,0:T(8,128)(2,1)}, u32[]{:S(2)}, u32[]{:S(2)}) collective-permute-start(bf16[144,512]{1,0:T(8,128)(2,1)} %get-tuple-element.243), channel_id=1, source_target_pairs={{2,0},{6,1},{3,2},{7,3},{0,4},{4,5},{1,6},{5,7},{10,8},{14,9},{11,... | collective-permute-start | bytes 442376 | tf_op jit(solution)/shard_map/ppermute | solution.py:396
  184.9 29.4 %collective-permute-start.34 = (bf16[144,512]{1,0:T(8,128)(2,1)}, bf16[144,512]{1,0:T(8,128)(2,1)}, u32[]{:S(2)}, u32[]{:S(2)}) collective-permute-start(bf16[144,512]{1,0:T(8,128)(2,1)} %get-tuple-element.244), channel_id=1, source_target_pairs={{1,0},{5,1},{0,2},{4,3},{3,4},{7,5},{2,6},{6,7},{9,8},{13,9},{8,10... | collective-permute-start | bytes 442376 | tf_op jit(solution)/shard_map/ppermute | solution.py:396
  239.4 108.1 %reduce-scatter.5.cloned.1.call-start = ((), (), s32[]{:S(2)}) async-start(), calls=%async_computation.2 | async-start | bytes 921600 | tf_op jit(solution)/shard_map/reduce_scatter | solution.py:605
  261.8 22.2 %collective-permute-start.41 = (bf16[4,576,576]{2,1,0:T(8,128)(2,1)}, bf16[4,576,576]{2,1,0:T(8,128)(2,1)}, u32[]{:S(2)}, u32[]{:S(2)}) collective-permute-start(bf16[4,576,576]{2,1,0:T(8,128)(2,1)} %get-tuple-element.121), channel_id=1, source_target_pairs={{0,1},{1,0},{2,3},{3,2},{4,5},{5,4},{6,7},{7,6},{8,9},{9,8},{10,11... | collective-permute-start | bytes 7962632 | tf_op jit(solution)/shard_map/ppermute | solution.py:253
  271.8 40.2 %collective-permute-start.42 = (bf16[144,768]{1,0:T(8,128)(2,1)}, bf16[144,768]{1,0:T(8,128)(2,1)}, u32[]{:S(2)}, u32[]{:S(2)}) collective-permute-start(bf16[144,768]{1,0:T(8,128)(2,1)} %get-tuple-element.207), channel_id=1, source_target_pairs={{0,2},{2,0},{4,6},{6,4},{1,3},{3,1},{5,7},{7,5},{8,10},{10,8},{12,... | collective-permute-start | bytes 663560 | tf_op jit(solution)/shard_map/ppermute | solution.py:253
  272.7 39.4 %collective-permute-start.44 = (bf16[144,768]{1,0:T(8,128)(2,1)}, bf16[144,768]{1,0:T(8,128)(2,1)}, u32[]{:S(2)}, u32[]{:S(2)}) collective-permute-start(bf16[144,768]{1,0:T(8,128)(2,1)} %get-tuple-element.208), channel_id=1, source_target_pairs={{0,6},{2,4},{4,2},{6,0},{1,7},{3,5},{5,3},{7,1},{8,14},{10,12},{12... | collective-permute-start | bytes 663560 | tf_op jit(solution)/shard_map/ppermute | solution.py:253
  275.9 36.1 %collective-permute-start.43 = (bf16[144,768]{1,0:T(8,128)(2,1)}, bf16[144,768]{1,0:T(8,128)(2,1)}, u32[]{:S(2)}, u32[]{:S(2)}) collective-permute-start(bf16[144,768]{1,0:T(8,128)(2,1)} %get-tuple-element.209), channel_id=1, source_target_pairs={{0,4},{2,6},{4,0},{6,2},{1,5},{3,7},{5,1},{7,3},{8,12},{10,14},{12... | collective-permute-start | bytes 663560 | tf_op jit(solution)/shard_map/ppermute | solution.py:253
  297.4 24.2 %collective-permute-start.45 = (bf16[2,576,576]{2,1,0:T(8,128)(2,1)}, bf16[2,576,576]{2,1,0:T(8,128)(2,1)}, u32[]{:S(2)}, u32[]{:S(2)}) collective-permute-start(bf16[2,576,576]{2,1,0:T(8,128)(2,1)} %slice.659), channel_id=1, source_target_pairs={{0,8},{1,17},{8,0},{9,25},{16,24},{17,1},{24,16},{25,9},{2,10},{3,... | collective-permute-start | bytes 3981320 | tf_op jit(solution)/shard_map/ppermute | solution.py:266
  321.5 24.0 %collective-permute-start.52 = (bf16[144,288]{0,1:T(8,128)(2,1)}, bf16[144,288]{0,1:T(8,128)(2,1)}, u32[]{:S(2)}, u32[]{:S(2)}) collective-permute-start(bf16[144,288]{0,1:T(8,128)(2,1)} %get-tuple-element.289), channel_id=1, source_target_pairs={{0,4},{2,6},{4,0},{6,2},{1,5},{3,7},{5,1},{7,3},{8,12},{10,14},{12... | collective-permute-start | bytes 248840 | tf_op jit(solution)/shard_map/ppermute | solution.py:253
  348.7 35.4 %collective-permute-start.54 = (bf16[144,1632]{1,0:T(8,128)(2,1)S(1)}, bf16[144,1632]{1,0:T(8,128)(2,1)S(1)}, u32[]{:S(2)}, u32[]{:S(2)}) collective-permute-start(bf16[144,1632]{1,0:T(8,128)(2,1)S(1)} %concatenate.294), channel_id=1, source_target_pairs={{0,16},{1,9},{8,24},{9,1},{16,0},{17,25},{24,8},{25,17},{2,18},{3,... | collective-permute-start | bytes 1410056 | tf_op jit(solution)/shard_map/ppermute | solution.py:266
  356.4 21.4 %collective-permute-start.61 = (bf16[144,488]{1,0:T(8,128)(2,1)S(1)}, bf16[144,488]{1,0:T(8,128)(2,1)S(1)}, u32[]{:S(2)}, u32[]{:S(2)}) collective-permute-start(bf16[144,488]{1,0:T(8,128)(2,1)S(1)} %get-tuple-element.232), channel_id=1, source_target_pairs={{0,4},{2,6},{4,0},{6,2},{1,5},{3,7},{5,1},{7,3},{8,12},{10,14},{12... | collective-permute-start | bytes 421640 | tf_op jit(solution)/shard_map/ppermute | solution.py:253
  393.1 24.4 %collective-permute-start.65 = (bf16[2,144,1632]{2,1,0:T(8,128)(2,1)S(1)}, bf16[2,144,1632]{2,1,0:T(8,128)(2,1)S(1)}, u32[]{:S(2)}, u32[]{:S(2)}) collective-permute-start(bf16[2,144,1632]{2,1,0:T(8,128)(2,1)S(1)} %pad_maximum_fusion.4), channel_id=1, source_target_pairs={{0,8},{1,17},{8,0},{9,25},{16,24},{17,1},{24,16},{25,9},{2,10},{3,... | collective-permute-start | bytes 2820104 | tf_op jit(solution)/shard_map/ppermute | solution.py:266
  (170 other events, 1153.7 us)
Sparse Core Ops, SparseCore 0:
  239.6 42.2 reduce-scatter.6
  314.7 30.6 reduce-scatter.4
where the time goes:
time: 441 us; the launch traced here: 433 us
  waiting for transfers between devices  90.4 us (20%)
  Pallas kernels  88.7 us (20%)
  starting transfers between devices  88.5 us (20%)
  local copies, waits for them, and re-layouts  63.1 us (14%)
  other arithmetic  57 us (13%)
  matrix products  27.4 us (6%)
  between operations  17.5 us (4%)
    ppermute x44, waiting for transfers between devices, swap(): return lax.ppermute(value, axis, [(i, i ^ distance) for i in range(count)])  65.8 us
    ppermute x44, starting transfers between devices, swap(): return lax.ppermute(value, axis, [(i, i ^ distance) for i in range(count)])  54.5 us
    unnamed x308, local copies, waits for them, and re-layouts  33.7 us
    pallas_call x4, Pallas kernels, ff_backward(): pl.pallas_call(functools.partial(ff_backward_kernel, part, chained), out_...  29.9 us
    dot_general x16, matrix products, dot(): lax.dot_general(left, right, (((left_dim,), (right_dim,)), ((), ())), pre...  27.4 us
    pallas_call x2, Pallas kernels, attend_back(): pl.pallas_call(backward_kernel, out_shape=(jax.ShapeDtypeStruct((H * HD,...  20.8 us
    pallas_call x2, Pallas kernels, attend(): pl.pallas_call(forward_kernel, out_shape=(jax.ShapeDtypeStruct((H * HD, t...  20.3 us
    pallas_call x2, Pallas kernels, ff_forward(): pl.pallas_call(functools.partial(ff_forward_kernel, part, count), out_sha...  17.7 us
  transfers between devices with their start and end apart: 70, of which 28 were waited for; matrix products, arithmetic and copies ran while one was open for 22% of the time, Pallas kernels for 16%

commit v1 on v0

--- a/solution.py
+++ b/solution.py
@@ -634,9 +634,6 @@
             ff_part = reduce_dp_second(ff_part)
         grad_kv = jnp.concatenate([grad_keys, grad_values], axis=0)
         kv_got = swap(grad_kv[:, tokens:].astype(BF), "col", 1)
-        if number == 0:
-            kv_got, out_sum = tie(kv_got, out_sum)
-            out_sum = reduce_rows(out_sum).astype(BF)
         grad_kv = grad_kv[:, :tokens] + kv_got.astype(F32)
         grad_query_raw = rotate(grad_query * HD**-0.5, cosine, -sine, H).astype(BF)
         grad_key_raw = rotate(grad_kv[: KVH * HD], cosine, -sine, KVH).astype(BF)
@@ -667,9 +664,15 @@
             )
             qkv_away, gain_all, gradient = tie(qkv_dot(1 - core, BF), gain_all, gradient)
             qkv_got = swap(jnp.concatenate([qkv_away, gain_all], axis=1), "col", 1)
-            early = jnp.concatenate([pending, attn_last, out_sum], axis=1)
+            early = jnp.concatenate([pending, attn_last], axis=1)
             qkv_own = jnp.concatenate([qkv_dot(core, F32), gain_all.astype(F32)], axis=1)
-            qkv_sum = reduce_rows(qkv_own + qkv_got.astype(F32))
+            qkv_sum = qkv_own + qkv_got.astype(F32)
+            gap = -qkv_sum.shape[1] % 128
+            qkv_sum = jnp.concatenate(
+                [qkv_sum, jnp.zeros((D, gap), F32), out_sum.astype(F32)], axis=1
+            )
+            out_begin = qkv_sum.shape[1] - q_width
+            qkv_sum = reduce_rows(qkv_sum)
             ff_total = reduce_rows(ff_part).astype(BF)
             ff_total, gradient, *early = tie(ff_total, gradient, *dp_first(early))
             ff_total = dp_gather(ff_total)
@@ -695,8 +698,8 @@
 
     first_total, middle_total = total_of(first_total), total_of(middle_total)
     attn_whole = [
-        jnp.concatenate([first_total[:, :qkv_col], middle_total[:, a_col:]], axis=1),
-        middle_total[:, :a_col],
+        jnp.concatenate([first_total[:, :qkv_col], first_total[:, out_begin:]], axis=1),
+        middle_total,
     ]
 
     def attn_of(number, begin, end):
@@ -705,7 +708,7 @@
     def stack(function):
         return jnp.stack([function(number) for number in range(layers)])
 
-    gain_total = first_total[:, qkv_col:]
+    gain_total = first_total[:, qkv_col : qkv_col + 4 * layers]
     gain_total = gain_total[:, : 2 * layers] + gain_total[:, 2 * layers :]
     gain_total = gain_total.T.reshape(layers, 2, -1)
 

time: 441 us -> 443 us (level)
    ppermute x44 -> x41, waiting for transfers between devices: 65.8 us -> 55.8 us  [swap(): return lax.ppermute(value, axis, [(i, i ^ distance) for i in range(count)])]
    ppermute x8, waiting for transfers between devices: 13.4 us -> 22 us  [dp_step(): return lax.ppermute(value, ('dp', 'col'), pairs)]
    reduce_scatter x1, waiting for transfers between devices: 0.01 us -> 6.86 us  [shards(): lax.psum_scatter(true_rows(pending), 'row', scatter_dimension=0, tiled=True)]
    unnamed x308 -> x310, local copies, waits for them, and re-layouts: 33.7 us -> 32 us
    ppermute x44 -> x41, starting transfers between devices: 54.5 us -> 53.2 us  [swap(): return lax.ppermute(value, axis, [(i, i ^ distance) for i in range(count)])]
  transfers between devices with their start and end apart: 70 -> 67, of which waited for: 28 -> 28; matrix products, arithmetic and copies ran while one was open for 22% -> 21% of each run, Pallas kernels for 16% -> 16%
where the time goes in v1:
time: 443 us; the launch traced here: 436 us
  waiting for transfers between devices  94.7 us (21%)
  starting transfers between devices  91.5 us (21%)
  Pallas kernels  89 us (20%)
  local copies, waits for them, and re-layouts  60.2 us (14%)
  other arithmetic  54.1 us (12%)
  matrix products  28.3 us (6%)
  between operations  17.7 us (4%)
    ppermute x41, waiting for transfers between devices, swap(): return lax.ppermute(value, axis, [(i, i ^ distance) for i in range(count)])  55.8 us
    ppermute x41, starting transfers between devices, swap(): return lax.ppermute(value, axis, [(i, i ^ distance) for i in range(count)])  53.2 us
    unnamed x310, local copies, waits for them, and re-layouts  32 us
    pallas_call x4, Pallas kernels, ff_backward(): pl.pallas_call(functools.partial(ff_backward_kernel, part, chained), out_...  29.9 us
    dot_general x16, matrix products, dot(): lax.dot_general(left, right, (((left_dim,), (right_dim,)), ((), ())), pre...  28.3 us
    ppermute x8, waiting for transfers between devices, dp_step(): return lax.ppermute(value, ('dp', 'col'), pairs)  22 us
    pallas_call x2, Pallas kernels, attend_back(): pl.pallas_call(backward_kernel, out_shape=(jax.ShapeDtypeStruct((H * HD,...  21 us
    pallas_call x2, Pallas kernels, attend(): pl.pallas_call(forward_kernel, out_shape=(jax.ShapeDtypeStruct((H * HD, t...  20.4 us
  transfers between devices with their start and end apart: 67, of which 28 were waited for; matrix products, arithmetic and copies ran while one was open for 21% of the time, Pallas kernels for 16%

profile of v1, /device:TPU:0, one launch (start us, length us, event | category | flops | bytes accessed | tf_op | source)
XLA Modules:
  0.0 435.6 jit_solution(3478040677812714146)
XLA Ops:
  11.9 5.1 %collective-permute-start.2 = (bf16[144,204]{0,1:T(8,128)(2,1)S(1)}, bf16[144,204]{0,1:T(8,128)(2,1)S(1)}, u32[]{:S(2)}, u32[]{:S(2)}) collective-permute-start(bf16[144,204]{0,1:T(8,128)(2,1)S(1)} %pad_maximum_fusion.46), channel_id=1, source_target_pairs={{0,6},{2,4},{4,2},{6,0},{1,7},{3,5},{5,3},{7,1},{8,14},{10,12},{12... | collective-permute-start | bytes 176264 | tf_op jit(solution)/shard_map/ppermute | solution.py:253
  18.8 4.6 %collective-permute-start.10 = (bf16[144,512]{1,0:T(8,128)(2,1)S(1)}, bf16[144,512]{1,0:T(8,128)(2,1)S(1)}, u32[]{:S(2)}, u32[]{:S(2)}) collective-permute-start(bf16[144,512]{1,0:T(8,128)(2,1)S(1)} %get-tuple-element.255), channel_id=1, source_target_pairs={{0,3},{1,7},{2,2},{3,6},{4,1},{5,5},{6,0},{7,4},{8,11},{9,15},{10,... | collective-permute-start | bytes 442376 | tf_op jit(solution)/shard_map/ppermute | solution.py:374
  35.8 7.8 %collective-permute-done.9 = bf16[144,512]{1,0:T(8,128)(2,1)S(1)} collective-permute-done((bf16[144,512]{1,0:T(8,128)(2,1)S(1)}, bf16[144,512]{1,0:T(8,128)(2,1)S(1)}, u32[]{:S(2)}, u32[]{:S(2)}) %collective-permute-start.9) | collective-permute-done | bytes 147488 | tf_op jit(solution)/shard_map/ppermute | solution.py:374
  70.8 10.4 %attend.2 = (f32[576,512]{1,0:T(8,128)S(1)}, bf16[576,512]{1,0:T(8,128)(2,1)S(1)}, f32[3,8,512]{2,1,0:T(8,128)S(1)}) custom-call(s32[1]{0:T(128)} %bitcast.core_ref, s32[1,512]{1,0:T(1,128)S(1)} %bitcast.339, bf16[576,512]{1,0:T(8,128)(2,1)S(1)} %bitcast.335, bf16[384,1024]{1,0:T(8,128)(2,1)S(1)} %pad_maximum_fusion.7.key_ref.value_ref, ...), custom_call_target="tpu_custom_call" | custom-call | flops 1207959552 | bytes 2359296 | tf_op jit(solution)/shard_map/attend/pallas_call | solution.py:71
  84.9 10.9 %collective-permute-done.20 = bf16[288,768]{1,0:T(8,128)(2,1)S(1)} collective-permute-done((bf16[288,768]{1,0:T(8,128)(2,1)S(1)}, bf16[288,768]{1,0:T(8,128)(2,1)S(1)}, u32[]{:S(2)}, u32[]{:S(2)}) %collective-permute-start.20) | collective-permute-done | bytes 442400 | tf_op jit(solution)/shard_map/ppermute | solution.py:253
  111.0 10.0 %ff_forward.2 = (f32[576,512]{1,0:T(8,128)S(1)}, f32[8,384,512]{2,1,0:T(8,128)}) custom-call(bf16[576,512]{1,0:T(8,128)(2,1)S(1)} %multiply_convert_fusion.2.normed_ref.refs_0_, f32[576,512]{1,0:T(8,128)S(1)} %convert_add_fusion.middle_ref, bf16[4,576,768]{2,1,0:T(8,128)(2,1)S(1)} %pad_maximum_fusion.near_ref.refs_3_, ...), custom_call_target="tpu_custom_call" | custom-call | flops 2717908992 | bytes 20971520 | tf_op jit(solution)/shard_map/ff_forward/pallas_call | solution.py:174
  123.3 4.3 concatenate.272
  135.6 6.5 %collective-permute-done.30 = bf16[288,576]{1,0:T(8,128)(2,1)S(1)} collective-permute-done((bf16[288,576]{1,0:T(8,128)(2,1)S(1)}, bf16[288,576]{1,0:T(8,128)(2,1)S(1)}, u32[]{:S(2)}, u32[]{:S(2)}) %collective-permute-start.30) | collective-permute-done | bytes 331808 | tf_op jit(solution)/shard_map/ppermute | solution.py:253
  151.7 10.0 %attend.3 = (f32[576,512]{1,0:T(8,128)S(1)}, bf16[576,512]{1,0:T(8,128)(2,1)S(1)}, f32[3,8,512]{2,1,0:T(8,128)S(1)}) custom-call(s32[1]{0:T(128)} %bitcast.core_ref, s32[1,512]{1,0:T(1,128)S(1)} %bitcast.340, bf16[576,512]{1,0:T(8,128)(2,1)S(1)} %bitcast.337, bf16[384,1024]{1,0:T(8,128)(2,1)S(1)} %pad_maximum_fusion.8.key_ref.value_ref, ...), custom_call_target="tpu_custom_call" | custom-call | flops 1207959552 | bytes 2359296 | tf_op jit(solution)/shard_map/attend/pallas_call | solution.py:71
  169.9 7.7 %ff_forward.3 = (f32[576,512]{1,0:T(8,128)S(1)}, f32[8,384,512]{2,1,0:T(8,128)}) custom-call(bf16[576,512]{1,0:T(8,128)(2,1)S(1)} %multiply_convert_fusion.normed_ref.refs_0_, f32[576,512]{1,0:T(8,128)S(1)} %get-tuple-element.335.middle_ref, bf16[4,576,576]{2,1,0:T(8,128)(2,1)S(1)} %pad_maximum_fusion.1.near_ref.refs_3_, ...), custom_call_target="tpu_custom_call" | custom-call | flops 2717908992 | bytes 20971520 | tf_op jit(solution)/shard_map/ff_forward/pallas_call | solution.py:174
  189.7 6.8 %ff_backward.4 = (f32[576,512]{1,0:T(8,128)S(1)}, bf16[4,576,576]{2,1,0:T(8,128)(2,1)}) custom-call(s32[4]{0:T(128)S(1)} %iota_xor_fusion.order_ref, bf16[576,512]{1,0:T(8,128)(2,1)S(1)} %multiply_convert_fusion.normed_ref.refs_0_, bf16[576,512]{1,0:T(8,128)(2,1)S(1)} %pad_maximum_fusion.19.refs_1_, f32[8,384,512]{2,1,0:T(8,128)S(1)} %copy-done, ...), custom_call_target="tpu_custom_call" | custom-call | flops 2717908992 | bytes 16777216 | tf_op jit(solution)/shard_map/ff_backward/pallas_call | solution.py:220
  196.5 7.0 %ff_backward.5 = (f32[576,512]{1,0:T(8,128)S(1)}, bf16[4,576,576]{2,1,0:T(8,128)(2,1)S(1)}) custom-call(s32[4]{0:T(128)S(1)} %iota_xor_fusion.order_ref, bf16[576,512]{1,0:T(8,128)(2,1)S(1)} %multiply_convert_fusion.normed_ref.refs_0_, bf16[576,512]{1,0:T(8,128)(2,1)S(1)} %pad_maximum_fusion.19.refs_1_, f32[8,384,512]{2,1,0:T(8,128)} %get-tuple-element.96.refs_2_, ...), custom_call_target="tpu_custom_call" | custom-call | flops 2717908992 | bytes 16777216 | tf_op jit(solution)/shard_map/ff_backward/pallas_call | solution.py:220
  217.0 4.2 add_convert_fusion.1
  226.5 10.4 %attend_back.2 = (f32[576,512]{1,0:T(8,128)S(1)}, f32[192,1024]{1,0:T(8,128)S(1)}, f32[192,1024]{1,0:T(8,128)S(1)}) custom-call(s32[1]{0:T(128)} %bitcast.core_ref, s32[1,512]{1,0:T(1,128)S(1)} %bitcast.341, bf16[576,512]{1,0:T(8,128)(2,1)S(1)} %bitcast.338, bf16[384,1024]{1,0:T(8,128)(2,1)S(1)} %copy-done.22, bf16[384,1024]{1,0:T(8,128)(2,1)S(1)} %copy-done.22, ...), custom_call_target="tpu_custom_call" | custom-call | flops 3019898880 | bytes 4718592 | tf_op jit(solution)/shard_map/attend_back/pallas_call | solution.py:127
  252.0 9.0 %ff_backward.6 = (f32[576,512]{1,0:T(8,128)S(1)}, bf16[4,576,576]{2,1,0:T(8,128)(2,1)}) custom-call(s32[4]{0:T(128)S(1)} %and_select_fusion.order_ref, bf16[576,512]{1,0:T(8,128)(2,1)S(1)} %copy-done.9, bf16[576,512]{1,0:T(8,128)(2,1)S(1)} %convert_element_type.333.refs_1_, f32[8,384,512]{2,1,0:T(8,128)} %get-tuple-element.111.refs_2_, ...), custom_call_target="tpu_custom_call" | custom-call | flops 2717908992 | bytes 16777216 | tf_op jit(solution)/shard_map/ff_backward/pallas_call | solution.py:220
  276.2 7.0 %ff_backward.7 = (f32[576,512]{1,0:T(8,128)S(1)}, bf16[4,576,576]{2,1,0:T(8,128)(2,1)S(1)}) custom-call(s32[4]{0:T(128)S(1)} %and_select_fusion.1.order_ref, bf16[576,512]{1,0:T(8,128)(2,1)S(1)} %copy-done.10, bf16[576,512]{1,0:T(8,128)(2,1)S(1)} %copy-done.7, f32[8,384,512]{2,1,0:T(8,128)} %get-tuple-element.111.refs_2_, ...), custom_call_target="tpu_custom_call" | custom-call | flops 2717908992 | bytes 16777216 | tf_op jit(solution)/shard_map/ff_backward/pallas_call | solution.py:220
  284.3 4.4 add_convert_fusion
  299.4 10.6 %attend_back.3 = (f32[576,512]{1,0:T(8,128)S(1)}, f32[192,1024]{1,0:T(8,128)S(1)}, f32[192,1024]{1,0:T(8,128)S(1)}) custom-call(s32[1]{0:T(128)} %bitcast.core_ref, s32[1,512]{1,0:T(1,128)S(1)} %bitcast.342, bf16[576,512]{1,0:T(8,128)(2,1)S(1)} %bitcast.336, bf16[384,1024]{1,0:T(8,128)(2,1)S(1)} %copy-done.20, bf16[384,1024]{1,0:T(8,128)(2,1)S(1)} %copy-done.20, ...), custom_call_target="tpu_custom_call" | custom-call | flops 3019898880 | bytes 4718592 | tf_op jit(solution)/shard_map/attend_back/pallas_call | solution.py:127
  330.3 6.9 %reduce-scatter.5.cloned.1.call-done = bf16[144,576]{1,0:T(8,128)(2,1)} async-done(((bf16[576,576]{1,0:T(8,128)(2,1)}), bf16[144,576]{1,0:T(8,128)(2,1)}) %reduce-scatter.5.cloned.1.call-update) | async-done | bytes 165904 | tf_op jit(solution)/shard_map/reduce_scatter | solution.py:605
  347.1 7.0 %collective-permute-done.46 = bf16[576,576]{1,0:T(8,128)(2,1)S(1)} collective-permute-done((bf16[576,576]{1,0:T(8,128)(2,1)}, bf16[576,576]{1,0:T(8,128)(2,1)S(1)}, u32[]{:S(2)}, u32[]{:S(2)}) %collective-permute-start.46) | collective-permute-done | bytes 663584 | tf_op jit(solution)/shard_map/ppermute | solution.py:266
  358.6 8.8 %collective-permute-start.48 = (bf16[144,576]{1,0:T(8,128)(2,1)S(1)}, bf16[144,576]{1,0:T(8,128)(2,1)S(1)}, u32[]{:S(2)}, u32[]{:S(2)}) collective-permute-start(bf16[144,576]{1,0:T(8,128)(2,1)S(1)} %get-tuple-element.223), channel_id=1, source_target_pairs={{0,4},{2,6},{4,0},{6,2},{1,5},{3,7},{5,1},{7,3},{8,12},{10,14},{12... | collective-permute-start | bytes 497672 | tf_op jit(solution)/shard_map/ppermute | solution.py:253
  367.5 11.0 %collective-permute-done.58 = bf16[144,800]{1,0:T(8,128)(2,1)S(1)} collective-permute-done((bf16[144,800]{1,0:T(8,128)(2,1)S(1)}, bf16[144,800]{1,0:T(8,128)(2,1)S(1)}, u32[]{:S(2)}, u32[]{:S(2)}) %collective-permute-start.58) | collective-permute-done | bytes 230432 | tf_op jit(solution)/shard_map/ppermute | solution.py:253
  384.1 5.8 %collective-permute-start.55 = (bf16[144,512]{1,0:T(8,128)(2,1)S(1)}, bf16[144,512]{1,0:T(8,128)(2,1)S(1)}, u32[]{:S(2)}, u32[]{:S(2)}) collective-permute-start(bf16[144,512]{1,0:T(8,128)(2,1)S(1)} %get-tuple-element.227), channel_id=1, source_target_pairs={{3,0},{7,1},{2,2},{6,3},{1,4},{5,5},{0,6},{4,7},{11,8},{15,9},{10,... | collective-permute-start | bytes 442376 | tf_op jit(solution)/shard_map/ppermute | solution.py:396
  402.5 9.2 %collective-permute-done.64 = bf16[2,144,576]{2,1,0:T(8,128)(2,1)S(1)} collective-permute-done((bf16[2,144,576]{2,1,0:T(8,128)(2,1)S(1)}, bf16[2,144,576]{2,1,0:T(8,128)(2,1)S(1)}, u32[]{:S(2)}, u32[]{:S(2)}) %collective-permute-start.64) | collective-permute-done | bytes 331808 | tf_op jit(solution)/shard_map/ppermute | solution.py:266
  (670 shorter events, 232.5 us)
Async XLA Ops:
  7.2 281.4 %reduce-scatter.7.cloned.1.call-start = ((), (), s32[]{:S(2)}) async-start(), calls=%async_computation.3 | async-start | bytes 3686400
  30.0 28.8 %collective-permute-start.17 = (bf16[144,768]{1,0:T(8,128)(2,1)S(1)}, bf16[144,768]{1,0:T(8,128)(2,1)S(1)}, u32[]{:S(2)}, u32[]{:S(2)}) collective-permute-start(bf16[144,768]{1,0:T(8,128)(2,1)S(1)} %pad_maximum_fusion.36), channel_id=1, source_target_pairs={{0,6},{2,4},{4,2},{6,0},{1,7},{3,5},{5,3},{7,1},{8,14},{10,12},{12... | collective-permute-start | bytes 663560 | tf_op jit(solution)/shard_map/ppermute | solution.py:253
  58.8 24.9 %collective-permute-start.19 = (bf16[576,768]{1,0:T(8,128)(2,1)S(1)}, bf16[576,768]{1,0:T(8,128)(2,1)S(1)}, u32[]{:S(2)}, u32[]{:S(2)}) collective-permute-start(bf16[576,768]{1,0:T(8,128)(2,1)S(1)} %constant_dynamic-update-slice_fusion.5), channel_id=1, source_target_pairs={{0,16},{8,24},{16,0},{24,8},{1,17},{9,25},{17,1},{25,9},{2,18},{10... | collective-permute-start | bytes 2654216 | tf_op jit(solution)/shard_map/ppermute | solution.py:253
  60.4 23.3 %collective-permute-start.18 = (bf16[576,768]{1,0:T(8,128)(2,1)S(1)}, bf16[576,768]{1,0:T(8,128)(2,1)S(1)}, u32[]{:S(2)}, u32[]{:S(2)}) collective-permute-start(bf16[576,768]{1,0:T(8,128)(2,1)S(1)} %constant_dynamic-update-slice_fusion.5), channel_id=1, source_target_pairs={{0,8},{8,0},{16,24},{24,16},{1,9},{9,1},{17,25},{25,17},{2,10},{10... | collective-permute-start | bytes 2654216 | tf_op jit(solution)/shard_map/ppermute | solution.py:253
  143.8 26.1 %collective-permute-start.32 = (bf16[4,576,576]{2,1,0:T(8,128)(2,1)S(1)}, bf16[4,576,576]{2,1,0:T(8,128)(2,1)S(1)}, u32[]{:S(2)}, u32[]{:S(2)}) collective-permute-start(bf16[4,576,576]{2,1,0:T(8,128)(2,1)S(1)} %pad_maximum_fusion.1.near_ref.refs_3_), channel_id=1, source_target_pairs={{0,1},{1,0},{2,3},{3,2},{4,5},{5,4},{6,7},{7,6},{8,9},{9,8},{10,11... | collective-permute-start | bytes 7962632 | tf_op jit(solution)/shard_map/ppermute | solution.py:253
  145.1 24.6 %collective-permute-start.26 = (bf16[144,512]{1,0:T(8,128)(2,1)S(1)}, bf16[144,512]{1,0:T(8,128)(2,1)S(1)}, u32[]{:S(2)}, u32[]{:S(2)}) collective-permute-start(bf16[144,512]{1,0:T(8,128)(2,1)S(1)} %get-tuple-element.240), channel_id=1, source_target_pairs={{0,0},{1,4},{2,1},{3,5},{4,2},{5,6},{6,3},{7,7},{8,8},{9,12},{10,9... | collective-permute-start | bytes 442376 | tf_op jit(solution)/shard_map/ppermute | solution.py:374
  145.7 23.9 %collective-permute-start.29 = (bf16[144,512]{1,0:T(8,128)(2,1)S(1)}, bf16[144,512]{1,0:T(8,128)(2,1)S(1)}, u32[]{:S(2)}, u32[]{:S(2)}) collective-permute-start(bf16[144,512]{1,0:T(8,128)(2,1)S(1)} %get-tuple-element.241), channel_id=1, source_target_pairs={{0,3},{1,7},{2,2},{3,6},{4,1},{5,5},{6,0},{7,4},{8,11},{9,15},{10,... | collective-permute-start | bytes 442376 | tf_op jit(solution)/shard_map/ppermute | solution.py:374
  148.4 21.2 %collective-permute-start.28 = (bf16[144,512]{1,0:T(8,128)(2,1)S(1)}, bf16[144,512]{1,0:T(8,128)(2,1)S(1)}, u32[]{:S(2)}, u32[]{:S(2)}) collective-permute-start(bf16[144,512]{1,0:T(8,128)(2,1)S(1)} %get-tuple-element.242), channel_id=1, source_target_pairs={{0,2},{1,6},{2,3},{3,7},{4,0},{5,4},{6,1},{7,5},{8,10},{9,14},{10,... | collective-permute-start | bytes 442376 | tf_op jit(solution)/shard_map/ppermute | solution.py:374
  178.6 36.1 %collective-permute-start.33 = (bf16[144,512]{1,0:T(8,128)(2,1)}, bf16[144,512]{1,0:T(8,128)(2,1)}, u32[]{:S(2)}, u32[]{:S(2)}) collective-permute-start(bf16[144,512]{1,0:T(8,128)(2,1)} %get-tuple-element.232), channel_id=1, source_target_pairs={{0,0},{4,1},{1,2},{5,3},{2,4},{6,5},{3,6},{7,7},{8,8},{12,9},{9,10... | collective-permute-start | bytes 442376 | tf_op jit(solution)/shard_map/ppermute | solution.py:396
  181.5 33.1 %collective-permute-start.36 = (bf16[144,512]{1,0:T(8,128)(2,1)}, bf16[144,512]{1,0:T(8,128)(2,1)}, u32[]{:S(2)}, u32[]{:S(2)}) collective-permute-start(bf16[144,512]{1,0:T(8,128)(2,1)} %get-tuple-element.233), channel_id=1, source_target_pairs={{3,0},{7,1},{2,2},{6,3},{1,4},{5,5},{0,6},{4,7},{11,8},{15,9},{10,... | collective-permute-start | bytes 442376 | tf_op jit(solution)/shard_map/ppermute | solution.py:396
  184.8 29.8 %collective-permute-start.35 = (bf16[144,512]{1,0:T(8,128)(2,1)}, bf16[144,512]{1,0:T(8,128)(2,1)}, u32[]{:S(2)}, u32[]{:S(2)}) collective-permute-start(bf16[144,512]{1,0:T(8,128)(2,1)} %get-tuple-element.234), channel_id=1, source_target_pairs={{2,0},{6,1},{3,2},{7,3},{0,4},{4,5},{1,6},{5,7},{10,8},{14,9},{11,... | collective-permute-start | bytes 442376 | tf_op jit(solution)/shard_map/ppermute | solution.py:396
  184.9 29.7 %collective-permute-start.34 = (bf16[144,512]{1,0:T(8,128)(2,1)}, bf16[144,512]{1,0:T(8,128)(2,1)}, u32[]{:S(2)}, u32[]{:S(2)}) collective-permute-start(bf16[144,512]{1,0:T(8,128)(2,1)} %get-tuple-element.235), channel_id=1, source_target_pairs={{1,0},{5,1},{0,2},{4,3},{3,4},{7,5},{2,6},{6,7},{9,8},{13,9},{8,10... | collective-permute-start | bytes 442376 | tf_op jit(solution)/shard_map/ppermute | solution.py:396
  239.8 97.4 %reduce-scatter.5.cloned.1.call-start = ((), (), s32[]{:S(2)}) async-start(), calls=%async_computation.2 | async-start | bytes 921600 | tf_op jit(solution)/shard_map/reduce_scatter | solution.py:605
  262.1 22.2 %collective-permute-start.41 = (bf16[4,576,576]{2,1,0:T(8,128)(2,1)}, bf16[4,576,576]{2,1,0:T(8,128)(2,1)}, u32[]{:S(2)}, u32[]{:S(2)}) collective-permute-start(bf16[4,576,576]{2,1,0:T(8,128)(2,1)} %get-tuple-element.119), channel_id=1, source_target_pairs={{0,1},{1,0},{2,3},{3,2},{4,5},{5,4},{6,7},{7,6},{8,9},{9,8},{10,11... | collective-permute-start | bytes 7962632 | tf_op jit(solution)/shard_map/ppermute | solution.py:253
  272.1 40.2 %collective-permute-start.42 = (bf16[144,768]{1,0:T(8,128)(2,1)}, bf16[144,768]{1,0:T(8,128)(2,1)}, u32[]{:S(2)}, u32[]{:S(2)}) collective-permute-start(bf16[144,768]{1,0:T(8,128)(2,1)} %get-tuple-element.206), channel_id=1, source_target_pairs={{0,2},{2,0},{4,6},{6,4},{1,3},{3,1},{5,7},{7,5},{8,10},{10,8},{12,... | collective-permute-start | bytes 663560 | tf_op jit(solution)/shard_map/ppermute | solution.py:253
  273.0 39.2 %collective-permute-start.44 = (bf16[144,768]{1,0:T(8,128)(2,1)}, bf16[144,768]{1,0:T(8,128)(2,1)}, u32[]{:S(2)}, u32[]{:S(2)}) collective-permute-start(bf16[144,768]{1,0:T(8,128)(2,1)} %get-tuple-element.207), channel_id=1, source_target_pairs={{0,6},{2,4},{4,2},{6,0},{1,7},{3,5},{5,3},{7,1},{8,14},{10,12},{12... | collective-permute-start | bytes 663560 | tf_op jit(solution)/shard_map/ppermute | solution.py:253
  276.2 36.0 %collective-permute-start.43 = (bf16[144,768]{1,0:T(8,128)(2,1)}, bf16[144,768]{1,0:T(8,128)(2,1)}, u32[]{:S(2)}, u32[]{:S(2)}) collective-permute-start(bf16[144,768]{1,0:T(8,128)(2,1)} %get-tuple-element.208), channel_id=1, source_target_pairs={{0,4},{2,6},{4,0},{6,2},{1,5},{3,7},{5,1},{7,3},{8,12},{10,14},{12... | collective-permute-start | bytes 663560 | tf_op jit(solution)/shard_map/ppermute | solution.py:253
  338.3 45.1 %collective-permute-start.51 = (bf16[144,1344]{1,0:T(8,128)(2,1)S(1)}, bf16[144,1344]{1,0:T(8,128)(2,1)S(1)}, u32[]{:S(2)}, u32[]{:S(2)}) collective-permute-start(bf16[144,1344]{1,0:T(8,128)(2,1)S(1)} %pad_maximum_fusion.31), channel_id=1, source_target_pairs={{0,16},{1,9},{8,24},{9,1},{16,0},{17,25},{24,8},{25,17},{2,18},{3,... | collective-permute-start | bytes 1161224 | tf_op jit(solution)/shard_map/ppermute | solution.py:266
  345.9 32.6 %collective-permute-start.58 = (bf16[144,800]{1,0:T(8,128)(2,1)S(1)}, bf16[144,800]{1,0:T(8,128)(2,1)S(1)}, u32[]{:S(2)}, u32[]{:S(2)}) collective-permute-start(bf16[144,800]{1,0:T(8,128)(2,1)S(1)} %get-tuple-element.205), channel_id=1, source_target_pairs={{0,4},{2,6},{4,0},{6,2},{1,5},{3,7},{5,1},{7,3},{8,12},{10,14},{12... | collective-permute-start | bytes 691208 | tf_op jit(solution)/shard_map/ppermute | solution.py:253
  354.4 25.7 %collective-permute-start.47 = (bf16[144,576]{1,0:T(8,128)(2,1)S(1)}, bf16[144,576]{1,0:T(8,128)(2,1)S(1)}, u32[]{:S(2)}, u32[]{:S(2)}) collective-permute-start(bf16[144,576]{1,0:T(8,128)(2,1)S(1)} %get-tuple-element.221), channel_id=1, source_target_pairs={{0,2},{2,0},{4,6},{6,4},{1,3},{3,1},{5,7},{7,5},{8,10},{10,8},{12,... | collective-permute-start | bytes 497672 | tf_op jit(solution)/shard_map/ppermute | solution.py:253
  355.7 24.4 %collective-permute-start.49 = (bf16[144,576]{1,0:T(8,128)(2,1)S(1)}, bf16[144,576]{1,0:T(8,128)(2,1)S(1)}, u32[]{:S(2)}, u32[]{:S(2)}) collective-permute-start(bf16[144,576]{1,0:T(8,128)(2,1)S(1)} %get-tuple-element.222), channel_id=1, source_target_pairs={{0,6},{2,4},{4,2},{6,0},{1,7},{3,5},{5,3},{7,1},{8,14},{10,12},{12... | collective-permute-start | bytes 497672 | tf_op jit(solution)/shard_map/ppermute | solution.py:253
  358.6 24.6 %collective-permute-start.48 = (bf16[144,576]{1,0:T(8,128)(2,1)S(1)}, bf16[144,576]{1,0:T(8,128)(2,1)S(1)}, u32[]{:S(2)}, u32[]{:S(2)}) collective-permute-start(bf16[144,576]{1,0:T(8,128)(2,1)S(1)} %get-tuple-element.223), channel_id=1, source_target_pairs={{0,4},{2,6},{4,0},{6,2},{1,5},{3,7},{5,1},{7,3},{8,12},{10,14},{12... | collective-permute-start | bytes 497672 | tf_op jit(solution)/shard_map/ppermute | solution.py:253
  378.6 23.8 %collective-permute-start.60 = (bf16[144,800]{1,0:T(8,128)(2,1)S(1)}, bf16[144,800]{1,0:T(8,128)(2,1)S(1)}, u32[]{:S(2)}, u32[]{:S(2)}) collective-permute-start(bf16[144,800]{1,0:T(8,128)(2,1)S(1)} %fusion.15), channel_id=1, source_target_pairs={{0,16},{1,9},{8,24},{9,1},{16,0},{17,25},{24,8},{25,17},{2,18},{3,... | collective-permute-start | bytes 691208 | tf_op jit(solution)/shard_map/ppermute | solution.py:266
  395.5 25.0 %collective-permute-start.62 = (bf16[2,144,1344]{2,1,0:T(8,128)(2,1)S(1)}, bf16[2,144,1344]{2,1,0:T(8,128)(2,1)S(1)}, u32[]{:S(2)}, u32[]{:S(2)}) collective-permute-start(bf16[2,144,1344]{2,1,0:T(8,128)(2,1)S(1)} %pad_maximum_fusion.6), channel_id=1, source_target_pairs={{0,8},{1,17},{8,0},{9,25},{16,24},{17,1},{24,16},{25,9},{2,10},{3,... | collective-permute-start | bytes 2322440 | tf_op jit(solution)/shard_map/ppermute | solution.py:266
  (168 other events, 1104.1 us)
Sparse Core Ops, SparseCore 0:
  239.9 42.3 reduce-scatter.6
  314.9 22.2 reduce-scatter.4
